TPU v7x, 32 devices: a whole 2x2x4 slice. The times are simulated.
32 devices in a mesh: img: 4 (over y, x), txt: 8 (over z, core).
Axes of the slice: x: 2, y: 2, z: 4, core: 2. Of those that a mesh axis runs over, the one named last changes fastest.
Arguments:
- img_emb: bfloat16 [160, 1152], P(('img', 'txt')), may hold values from -6 to 6
- txt_emb: bfloat16 [160, 1152], P(('img', 'txt')), may hold values from -6 to 6
- match: int32 [160], P(('img', 'txt')), may hold values from 0 to 159, each once
- log_temp: float32 [1], replicated, may hold values from 1.6 to 2.6
- bias: float32 [1], replicated, may hold values from -4 to -2
Outputs:
- grad_img: float32 [160, 1152], P(('img', 'txt'))
- grad_txt: float32 [160, 1152], P(('img', 'txt'))
- loss: float32 [1], replicated
- grad_log_temp: float32 [1], replicated
- grad_bias: float32 [1], replicated
Inputs may be any that keep to these rules, and one draw needn't show every extreme that they name: match is a permutation of the text rows.
All inputs are finite; a program needn't handle non-finite values.
Results may differ from a plain program's by a relative error of at most 0.0042.
Values may be sent and summed in bfloat16 or wider, within the bound.
A program may use at most 64 MiB of HBM per device.

v0:
```python
import jax
import jax.numpy as jnp
from jax import lax
from jax.sharding import PartitionSpec as P


def unit_rows(values):
    wide = values.astype(jnp.float32)
    length = jnp.sqrt(jnp.sum(wide * wide, axis=-1, keepdims=True) + 1e-06)
    return (wide / length, length)


def unit_back(unit, length, upstream):
    return (upstream - unit * jnp.sum(unit * upstream, axis=-1, keepdims=True)) / length


def per_device(img_emb, txt_emb, match, log_temp, bias):
    img_unit, img_norm = unit_rows(img_emb)
    txt_unit, txt_norm = unit_rows(txt_emb)
    img_cast = img_unit.astype(jnp.bfloat16)
    txt_cast = txt_unit.astype(jnp.bfloat16)
    img_rows, img_match = (
        lax.all_gather(img_cast, "txt", axis=0, tiled=True),
        lax.all_gather(match, "txt", axis=0, tiled=True),
    )
    txt_rows = lax.all_gather(txt_cast, "img", axis=0, tiled=True)
    temper = jnp.exp(log_temp[0])
    offset = bias[0]
    own_rows = txt_emb.shape[0]
    txt_count = lax.axis_size("txt")
    img_count = lax.axis_size("img")
    txt_place = lax.axis_index("txt")
    products = lax.dot_general(
        img_rows, txt_rows, (((1,), (1,)), ((), ())), preferred_element_type=jnp.float32
    )
    column = jnp.arange(txt_rows.shape[0], dtype=jnp.int32)
    global_col = (column // own_rows * txt_count + txt_place) * own_rows + column % own_rows
    label_sign = jnp.where(img_match[:, None] == global_col[None, :], 1.0, -1.0).astype(jnp.float32)
    scaled = temper * products
    logits = scaled + offset
    slopes = -label_sign * jax.nn.sigmoid(-label_sign * logits)
    partial_value = jnp.stack(
        [jnp.sum(jax.nn.softplus(-label_sign * logits)), jnp.sum(slopes), jnp.sum(slopes * scaled)]
    )
    weighted = (temper * slopes).astype(jnp.bfloat16)
    img_term = jnp.dot(weighted, txt_rows, preferred_element_type=jnp.float32)
    grad_img_unit = lax.psum_scatter(img_term, "txt", scatter_dimension=0, tiled=True)
    grad_txt_unit = lax.psum_scatter(
        lax.dot_general(
            weighted, img_rows, (((0,), (0,)), ((), ())), preferred_element_type=jnp.float32
        ),
        "img",
        scatter_dimension=0,
        tiled=True,
    )
    totals = lax.psum(partial_value, ("img", "txt"))
    batch_size = jnp.float32(own_rows * img_count * txt_count)
    totals = totals / (batch_size * batch_size)
    grad_img = unit_back(img_unit, img_norm, grad_img_unit)
    grad_txt = unit_back(txt_unit, txt_norm, grad_txt_unit)
    return (grad_img, grad_txt, totals[0:1], totals[2:3], totals[1:2])


def solution(mesh):
    return jax.shard_map(
        per_device,
        mesh=mesh,
        in_specs=(P(("img", "txt"), None), P(("img", "txt"), None), P(("img", "txt")), P(), P()),
        out_specs=(P(("img", "txt"), None), P(("img", "txt"), None), P(), P(), P()),
        check_vma=False,
    )
```

profile of v0, /device:TPU:0, one launch (start us, length us, event | category | flops | bytes accessed | tf_op | source)
XLA Modules:
  0.0 151.6 jit_solution(16170130421377828241)
XLA Ops:
  7.2 0.0 copy-start.1
  7.2 0.0 all-reduce.8.cloned.1.call-start
  7.2 0.0 copy-start
  8.6 0.0 copy-done.1
  8.6 0.1 fusion
  8.7 0.0 copy-done
  8.8 0.1 fusion.1
  8.9 0.0 copy-start.2
  8.9 0.6 copy-done.2
  9.6 0.6 fusion.11
  10.8 0.0 copy-start.3
  10.8 0.6 copy-done.3
  11.5 0.2 dynamic-update-slice
  11.6 10.6 %all-reduce = s32[40]{0:T(128)S(1)} all-reduce(s32[40]{0:T(128)S(1)} %dynamic-update-slice), channel_id=1, replica_groups=mesh['img'=4,'txt'=8] {'txt'}, use_global_device_ids=true, to_apply=%add | all-reduce | flops 40 | bytes 320
  22.2 0.1 convert_bitcast_fusion
  22.3 0.1 convert_bitcast_fusion.1
  22.4 8.3 %all-gather.1 = bf16[4,5,1152]{2,1,0:T(8,128)(2,1)S(1)} all-gather(bf16[1,5,1152]{2,1,0:T(8,128)(2,1)S(1)} %convert_bitcast_fusion), channel_id=1, replica_groups=mesh['img'=4,'txt'=8] {'img'}, dimensions={0}, use_global_device_ids=true | all-gather | bytes 57600 | tf_op jit(solution)/shard_map/all_gather | solution.py:26
  30.7 14.0 %all-gather = bf16[8,5,1152]{2,1,0:T(8,128)(2,1)S(1)} all-gather(bf16[1,5,1152]{2,1,0:T(8,128)(2,1)S(1)} %convert_bitcast_fusion.1), channel_id=1, replica_groups=mesh['img'=4,'txt'=8] {'txt'}, dimensions={0}, use_global_device_ids=true | all-gather | bytes 103680 | tf_op jit(solution)/shard_map/all_gather | solution.py:23
  44.8 0.9 fusion.2
  45.6 0.9 fusion.3
  46.5 0.0 all-reduce.8.cloned.1.call-update
  46.5 0.0 all-reduce.6.cloned.1.call-start
  46.6 1.0 fusion.4
  47.6 0.0 copy-start.4
  47.6 0.0 all-reduce.6.cloned.1.call-update
  47.6 0.6 copy-done.4
  48.2 0.6 dynamic-slice.3
  49.5 2.0 %pad_maximum_fusion = f32[3]{0:T(128)S(1)} fusion(f32[1]{0:T(128)} %bitcast.7, f32[1]{0:T(128)} %bitcast.6, f32[1]{0:T(128)} %bitcast.5), kind=kLoop, calls=%fused_computation.31 | loop fusion | flops 6 | bytes 24 | tf_op jit(solution)/shard_map/stack | solution.py:42
  52.2 37.7 %psum.7 = f32[3]{0:T(128)S(1)} all-reduce(f32[3]{0:T(128)S(1)} %pad_maximum_fusion), channel_id=1, replica_groups=mesh['img'=4,'txt'=8] {'img','txt'}, use_global_device_ids=true, to_apply=%region_9.10 | all-reduce | flops 3 | bytes 24 | tf_op jit(solution)/shard_map/psum | solution.py:56
  89.8 0.6 fusion.10
  90.4 0.0 all-reduce.8.cloned.1.call-done
  90.4 1.1 multiply_reduce_fusion
  91.5 1.6 %subtract_divide_fusion = f32[5,1152]{1,0:T(8,128)} fusion(f32[20,1152]{1,0:T(8,128)} %all-reduce.8.cloned.1.call-done, u32[]{:T(128)S(6)} %multiply.7, f32[5]{0:T(128)S(1)} %multiply_reduce_fusion, f32[5]{0:T(128)S(1)} %add_sqrt_fusion, bf16[5,1152]{1,0:T(8,128)(2,1)S(1)} %copy-done), kind=kLoop, calls=%fused_computation.7 | loop fusion | flops 28800 | bytes 57644 | tf_op jit(solution)/shard_map/div | solution.py:14
  93.1 49.0 %all-reduce.6.cloned.1.call-done = f32[40,1152]{1,0:T(8,128)} async-done(((f32[40,1152]{1,0:T(8,128)}), f32[40,1152]{1,0:T(8,128)}) %all-reduce.6.cloned.1.call-update) | async-done | bytes 184336
  142.1 1.1 multiply_reduce_fusion.1
  143.2 1.6 %subtract_divide_fusion.1 = f32[5,1152]{1,0:T(8,128)} fusion(f32[40,1152]{1,0:T(8,128)} %all-reduce.6.cloned.1.call-done, u32[]{:T(128)S(6)} %multiply.5, f32[5]{0:T(128)S(1)} %multiply_reduce_fusion.1, f32[5]{0:T(128)S(1)} %add_sqrt_fusion.1, bf16[5,1152]{1,0:T(8,128)(2,1)S(1)} %copy-done.1), kind=kLoop, calls=%fused_computation.9 | loop fusion | flops 28800 | bytes 57644 | tf_op jit(solution)/shard_map/div | solution.py:14
  (7 shorter events, 0.1 us)
Async XLA Ops:
  7.2 1.4 copy-start.1
  7.2 83.2 %all-reduce.8.cloned.1.call-start = ((), (), s32[]{:S(2)}) async-start(), calls=%async_computation.1 | async-start | bytes 221184
  7.2 1.5 %copy-start = (bf16[5,1152]{1,0:T(8,128)(2,1)S(1)}, bf16[5,1152]{1,0:T(8,128)(2,1)}, u32[]{:S(2)}) copy-start(bf16[5,1152]{1,0:T(8,128)(2,1)} %param.6) | copy-start | bytes 34564
  8.9 0.7 copy-start.2
  10.8 0.7 copy-start.3
  46.5 95.6 %all-reduce.6.cloned.1.call-start = ((), (), s32[]{:S(2)}) async-start(), calls=%async_computation | async-start | bytes 368640
  47.6 0.7 copy-start.4
Sparse Core Ops, SparseCore 0:
  46.6 38.8 all-reduce.7
  88.0 54.0 all-reduce.5
where the time goes:
time: 152 us
  blocking collectives  70.6 us (46%)
  waiting for transfers between devices  49.1 us (32%)
  between operations  17.4 us (11%)
  other arithmetic  7.81 us (5%)
  local copies, waits for them, and re-layouts  3.95 us (3%)
  matrix products  2.7 us (2%)
    unnamed x4, waiting for transfers between devices  49.1 us
    psum x1, blocking collectives, per_device(): totals = lax.psum(partial_value, ('img', 'txt'))  37.7 us
    all_gather x1, blocking collectives, per_device(): lax.all_gather(img_cast, 'txt', axis=0, tiled=True)  14 us
    unnamed x1, blocking collectives  10.6 us
    all_gather x1, blocking collectives, per_device(): txt_rows = lax.all_gather(txt_cast, 'img', axis=0, tiled=True)  8.31 us
    unnamed x16, local copies, waits for them, and re-layouts  3.36 us
    div x2, other arithmetic, unit_back(): (upstream - unit * jnp.sum(unit * upstream, axis=-1, keepdims=True)) / le...  3.18 us
  transfers between devices with their start and end apart: 2, of which 1 were waited for; matrix products, arithmetic and copies ran while one was open for 5% of the time, Pallas kernels for 0%

commit v1 on v0

v1 whole, which is shorter than its diff:
```python
import functools

import jax
import jax.numpy as jnp
from jax import lax
from jax.experimental import pallas as pl
from jax.experimental.pallas import tpu as pltpu
from jax.sharding import PartitionSpec as P

MESH = pl.DeviceIdType.MESH
PAD = 8
DIGIT = 64


def each(start, stop, body):
    if stop - start <= 32:
        for k in range(start, stop):
            body(k)
    else:
        lax.fori_loop(start, stop, lambda k, c: (body(k), c)[1], 0)


def kernel(
    n_img, n_txt,
    img_hbm, txt_hbm, match_ref, temp_ref, bias_ref,
    grad_img_ref, grad_txt_ref, loss_ref, dtemp_ref, dbias_ref,
    img_in, txt_in, img_all, txt_all, img_part, txt_part, img_back, txt_back, sums,
    in_sem, img_out, txt_out, txt_back_out, img_back_out, sums_out, img_sem, txt_sem, img_back_sem, txt_back_sem, sums_sem,
):
    rows, width = img_in.shape
    n_z = n_txt // 2
    n_plane = n_img * 2
    n_all = n_img * n_txt
    i = lax.axis_index("img")
    t = lax.axis_index("txt")
    z, core = t // 2, t % 2
    me = i * n_txt + t

    def plane(k, sign):
        return (
            lax.rem(i + sign * (k // 2) + n_img, n_img),
            z * 2 + lax.rem(core + k, 2),
        )

    def column(k, sign):
        return (i, lax.rem(z + sign * k + n_z, n_z) * 2 + core)

    def anyone(k):
        other = lax.rem(me + k, n_all)
        return (other // n_txt, lax.rem(other, n_txt))

    load_img = pltpu.make_async_copy(img_hbm, img_in, in_sem.at[0])
    load_txt = pltpu.make_async_copy(txt_hbm, txt_in, in_sem.at[1])
    load_img.start()
    load_txt.start()

    barrier = pltpu.get_barrier_semaphore()
    each(1, n_all, lambda k: pl.semaphore_signal(
        barrier, inc=1, device_id=anyone(k), device_id_type=MESH))

    def unit_rows(ref):
        wide = ref[...].astype(jnp.float32)
        norm = jnp.sqrt(jnp.sum(wide * wide, axis=-1, keepdims=True) + 1e-06)
        return wide / norm, norm

    load_img.wait()
    img_unit, img_norm = unit_rows(img_in)
    sub = lax.broadcasted_iota(jnp.int32, (PAD - rows, width), 0)
    lane = lax.broadcasted_iota(jnp.int32, (PAD - rows, width), 1)
    digits = jnp.zeros((PAD - rows, width), jnp.int32)
    for r in range(rows):
        m = match_ref[r]
        high = m // DIGIT
        digit = jnp.where(sub == 0, high, jnp.where(sub == 1, m - high * DIGIT, 0))
        digits = jnp.where(lane == r, digit, digits)
    img_all[0] = jnp.concatenate([img_unit, digits.astype(jnp.float32)], axis=0).astype(jnp.bfloat16)
    load_txt.wait()
    txt_unit, txt_norm = unit_rows(txt_in)
    txt_all[0] = jnp.concatenate(
        [txt_unit, jnp.zeros((PAD - rows, width), jnp.float32)], axis=0).astype(jnp.bfloat16)

    pl.semaphore_wait(barrier, n_all - 1)

    def img_copy(k):
        return pltpu.make_async_remote_copy(
            src_ref=img_all.at[0], dst_ref=img_all.at[k], send_sem=img_out.at[k],
            recv_sem=img_sem.at[k], device_id=plane(k, 1), device_id_type=MESH)

    def txt_copy(k):
        return pltpu.make_async_remote_copy(
            src_ref=txt_all.at[0], dst_ref=txt_all.at[k], send_sem=txt_out.at[k],
            recv_sem=txt_sem.at[k], device_id=column(k, 1), device_id_type=MESH)

    each(1, n_z, lambda k: txt_copy(k).start())
    each(1, n_plane, lambda k: img_copy(k).start())

    each(1, n_z, lambda k: txt_copy(k).wait_recv())
    each(1, n_plane, lambda k: img_copy(k).wait_recv())

    n_rows, n_cols = n_plane * PAD, n_z * PAD
    img_rows = img_all[...].astype(jnp.float32).reshape(n_rows, width).astype(jnp.bfloat16)
    txt_rows = txt_all[...].astype(jnp.float32).reshape(n_cols, width).astype(jnp.bfloat16)
    products = lax.dot_general(
        img_rows, txt_rows, (((1,), (1,)), ((), ())), preferred_element_type=jnp.float32)

    head = img_all[:, :, 0:128].astype(jnp.float32)
    whole = head[:, rows:rows + 1, :] * float(DIGIT) + head[:, rows + 1:rows + 2, :]
    spot = lax.broadcasted_iota(jnp.int32, (n_plane, PAD, 128), 1)
    at = lax.broadcasted_iota(jnp.int32, (n_plane, PAD, 128), 2)
    labels = jnp.sum(
        jnp.where(spot == at, jnp.broadcast_to(whole, (n_plane, PAD, 128)), 0.0),
        axis=-1, keepdims=True).reshape(n_rows, 1)

    row = lax.broadcasted_iota(jnp.int32, (n_rows, n_cols), 0)
    col = lax.broadcasted_iota(jnp.int32, (n_rows, n_cols), 1)
    slot = col // PAD
    place = lax.rem(z - slot + n_z, n_z) * 2 + core
    global_col = (i * n_txt + place) * rows + col % PAD
    valid = (row % PAD < rows) & (col % PAD < rows)
    sign = jnp.where(labels == global_col.astype(jnp.float32), 1.0, -1.0)

    temper = jnp.exp(jnp.full((1, 1), temp_ref[0], jnp.float32))
    scaled = temper * products
    margin = sign * (scaled + bias_ref[0])
    small = jnp.exp(-jnp.abs(margin))
    pair_loss = jnp.maximum(-margin, 0.0) + jnp.log1p(small)
    slopes = jnp.where(valid, -sign * jnp.where(margin >= 0.0, small, 1.0) / (1.0 + small), 0.0)
    pair_loss = jnp.where(valid, pair_loss, 0.0)

    def total(values):
        return jnp.sum(jnp.sum(values, axis=0, keepdims=True), axis=1, keepdims=True)

    lane = lax.broadcasted_iota(jnp.int32, (1, 128), 1)
    sums[0] = jnp.where(
        lane == 0, total(pair_loss),
        jnp.where(lane == 1, total(slopes * scaled), jnp.where(lane == 2, total(slopes), 0.0)))

    def sums_copy(k):
        return pltpu.make_async_remote_copy(
            src_ref=sums.at[0], dst_ref=sums.at[k], send_sem=sums_out.at[k],
            recv_sem=sums_sem.at[k], device_id=anyone(k), device_id_type=MESH)

    weighted = (temper * slopes).astype(jnp.bfloat16)
    txt_term = lax.dot_general(
        weighted, img_rows, (((0,), (0,)), ((), ())), preferred_element_type=jnp.float32)
    txt_part[...] = txt_term.reshape(n_z, PAD, width).astype(jnp.bfloat16)

    def txt_back_copy(k):
        return pltpu.make_async_remote_copy(
            src_ref=txt_part.at[k], dst_ref=txt_back.at[k], send_sem=txt_back_out.at[k],
            recv_sem=txt_back_sem.at[k], device_id=column(k, -1), device_id_type=MESH)

    each(1, n_z, lambda k: txt_back_copy(k).start())

    img_term = jnp.dot(weighted, txt_rows, preferred_element_type=jnp.float32)
    img_part[...] = img_term.reshape(n_plane, PAD, width).astype(jnp.bfloat16)

    def img_back_copy(k):
        return pltpu.make_async_remote_copy(
            src_ref=img_part.at[k], dst_ref=img_back.at[k], send_sem=img_back_out.at[k],
            recv_sem=img_back_sem.at[k], device_id=plane(k, -1), device_id_type=MESH)

    each(1, n_plane, lambda k: img_back_copy(k).start())
    each(1, n_all, lambda k: sums_copy(k).start())

    def unit_back(unit, norm, upstream):
        return (upstream - unit * jnp.sum(unit * upstream, axis=-1, keepdims=True)) / norm

    def gather_sum(own, back, n, copy):
        each(1, n, lambda k: copy(k).wait_recv())
        return (own + jnp.sum(back[1:].astype(jnp.float32), axis=0))[0:rows]

    grad_txt_unit = gather_sum(txt_term[0:PAD], txt_back, n_z, txt_back_copy)
    grad_txt_ref[...] = unit_back(txt_unit, txt_norm, grad_txt_unit)
    grad_img_unit = gather_sum(img_term[0:PAD], img_back, n_plane, img_back_copy)
    grad_img_ref[...] = unit_back(img_unit, img_norm, grad_img_unit)

    each(1, n_all, lambda k: sums_copy(k).wait_recv())
    batch = jnp.float32(rows * n_all)
    totals = jnp.sum(sums[...], axis=0) / (batch * batch)
    loss_ref[0] = jnp.sum(jnp.where(lane == 0, totals, 0.0))
    dtemp_ref[0] = jnp.sum(jnp.where(lane == 1, totals, 0.0))
    dbias_ref[0] = jnp.sum(jnp.where(lane == 2, totals, 0.0))

    each(1, n_z, lambda k: (txt_copy(k).wait_send(), txt_back_copy(k).wait_send()))
    each(1, n_plane, lambda k: (img_copy(k).wait_send(), img_back_copy(k).wait_send()))
    each(1, n_all, lambda k: sums_copy(k).wait_send())


def solution(mesh):
    n_img, n_txt = mesh.shape["img"], mesh.shape["txt"]
    n_z, n_plane, n_all = n_txt // 2, n_img * 2, n_img * n_txt

    def per_device(img_emb, txt_emb, match, log_temp, bias):
        rows, width = img_emb.shape
        smem = pl.BlockSpec(memory_space=pltpu.SMEM)
        vmem = pl.BlockSpec(memory_space=pltpu.VMEM)
        hbm = pl.BlockSpec(memory_space=pl.ANY)
        one = jax.ShapeDtypeStruct((1,), jnp.float32)
        grad = jax.ShapeDtypeStruct((rows, width), jnp.float32)
        dma = pltpu.SemaphoreType.DMA
        return pl.pallas_call(
            functools.partial(kernel, n_img, n_txt),
            out_shape=(grad, grad, one, one, one),
            in_specs=[hbm, hbm, smem, smem, smem],
            out_specs=(vmem, vmem, smem, smem, smem),
            scratch_shapes=[
                pltpu.VMEM((rows, width), jnp.bfloat16),
                pltpu.VMEM((rows, width), jnp.bfloat16),
                pltpu.VMEM((n_plane, PAD, width), jnp.bfloat16),
                pltpu.VMEM((n_z, PAD, width), jnp.bfloat16),
                pltpu.VMEM((n_plane, PAD, width), jnp.bfloat16),
                pltpu.VMEM((n_z, PAD, width), jnp.bfloat16),
                pltpu.VMEM((n_plane, PAD, width), jnp.bfloat16),
                pltpu.VMEM((n_z, PAD, width), jnp.bfloat16),
                pltpu.VMEM((n_all, 1, 128), jnp.float32),
                dma((2,)),
                dma((n_plane,)),
                dma((n_z,)),
                dma((n_z,)),
                dma((n_plane,)),
                dma((n_all,)),
                dma((n_plane,)),
                dma((n_z,)),
                dma((n_plane,)),
                dma((n_z,)),
                dma((n_all,)),
            ],
            compiler_params=pltpu.CompilerParams(
                collective_id=0, has_side_effects=True, vmem_limit_bytes=40 * 1024 * 1024),
        )(img_emb, txt_emb, match, log_temp, bias)

    split = P(("img", "txt"), None)
    return jax.shard_map(
        per_device,
        mesh=mesh,
        in_specs=(split, split, P(("img", "txt")), P(), P()),
        out_specs=(split, split, P(), P(), P()),
        check_vma=False,
    )
```

time: 152 us -> 28.5 us (0.19)
  blocking collectives: 70.6 us -> 0 us
  waiting for transfers between devices: 49.1 us -> 0 us
  Pallas kernels: 0 us -> 18.4 us
  between operations: 17.4 us -> 7.14 us
  other arithmetic: 7.81 us -> 0 us
  matrix products: 2.7 us -> 0 us
    unnamed x4 -> x0, waiting for transfers between devices: 49.1 us -> none
    psum x1 -> x0, blocking collectives: 37.7 us -> none  [per_device(): totals = lax.psum(partial_value, ('img', 'txt'))]
    all_gather x2 -> x0, blocking collectives: 22.3 us -> none  [the longest x1 14 us: per_device(): lax.all_gather(img_cast, 'txt', axis=0, tiled=True)]
    pallas_call x0 -> x1, Pallas kernels: none -> 18.4 us  [per_device(): pl.pallas_call(functools.partial(kernel, n_img, n_txt), out_shape=(grad,...]
    unnamed x1 -> x0, blocking collectives: 10.6 us -> none
    div x3 -> x0, other arithmetic: 3.18 us -> none  [the longest x2 3.18 us: unit_back(): (upstream - unit * jnp.sum(unit * upstream, axis=-1, keepdims=True)) / le...]
    dot_general x3 -> x0, matrix products: 2.7 us -> none  [the longest x1 0.98 us: per_device(): img_term = jnp.dot(weighted, txt_rows, preferred_element_type=jnp.float32)]
    reduce_sum x4 -> x0, other arithmetic: 2.4 us -> none  [the longest x2 2.15 us: unit_back(): jnp.sum(unit * upstream, axis=-1, keepdims=True)]
  transfers between devices with their start and end apart: 2 -> 0, of which waited for: 1 -> 0; matrix products, arithmetic and copies ran while one was open for 5% -> 0% of each run, Pallas kernels for 0% -> 0%
where the time goes in v1:
time: 28.5 us; the launch traced here: 28.2 us
  Pallas kernels  18.4 us (65%)
  between operations  7.14 us (25%)
  local copies, waits for them, and re-layouts  2.68 us (9%)
    pallas_call x1, Pallas kernels, per_device(): pl.pallas_call(functools.partial(kernel, n_img, n_txt), out_shape=(grad,...  18.4 us
    unnamed x8, local copies, waits for them, and re-layouts  2.68 us

profile of v1, /device:TPU:0, one launch (start us, length us, event | category | flops | bytes accessed | tf_op | source)
XLA Modules:
  0.0 28.2 jit_solution(288187280072105718)
XLA Ops:
  1.3 0.0 copy-start.2
  1.9 0.0 copy-done.2
  2.0 0.0 copy-start
  2.0 0.7 %copy-done = bf16[5,1152]{1,0:T(8,128)(2,1)S(1)} copy-done((bf16[5,1152]{1,0:T(8,128)(2,1)S(1)}, bf16[5,1152]{1,0:T(8,128)(2,1)}, u32[]{:S(2)}) %copy-start) | copy-done | bytes 11544
  2.7 0.0 copy-start.1
  2.7 0.7 %copy-done.1 = bf16[5,1152]{1,0:T(8,128)(2,1)S(1)} copy-done((bf16[5,1152]{1,0:T(8,128)(2,1)S(1)}, bf16[5,1152]{1,0:T(8,128)(2,1)}, u32[]{:S(2)}) %copy-start.1) | copy-done | bytes 11544
  3.4 18.4 %shard_map.92 = (f32[5,1152]{1,0:T(8,128)S(1)}, f32[5,1152]{1,0:T(8,128)S(1)}, f32[1]{0:T(128)}, f32[1]{0:T(128)}, f32[1]{0:T(128)}) custom-call(bf16[5,1152]{1,0:T(8,128)(2,1)S(1)} %copy-done, bf16[5,1152]{1,0:T(8,128)(2,1)S(1)} %copy-done.1, s32[5]{0:T(128)S(1)} %copy-done.2, f32[1]{0:T(128)S(6)} %copy.15.temp_ref, f32[1]{0:T(128)S(6)} %copy.16.bias_ref), custom_call_target="tpu_custom_call" | custom-call | tf_op jit(solution)/shard_map/pallas_call | solution.py:202
  21.8 0.6 %copy.17 = f32[5,1152]{1,0:T(8,128)} copy(f32[5,1152]{1,0:T(8,128)S(1)} %get-tuple-element.10) | data formatting | bytes 46080
  22.4 0.6 %copy.18 = f32[5,1152]{1,0:T(8,128)} copy(f32[5,1152]{1,0:T(8,128)S(1)} %get-tuple-element.11) | data formatting | bytes 46080
Async XLA Ops:
  1.3 0.7 %copy-start.2 = (s32[5]{0:T(128)S(1)}, s32[5]{0:T(128)}, u32[]{:S(2)}) copy-start(s32[5]{0:T(128)} %match_ref.1) | copy-start | bytes 64
  2.0 0.7 %copy-start = (bf16[5,1152]{1,0:T(8,128)(2,1)S(1)}, bf16[5,1152]{1,0:T(8,128)(2,1)}, u32[]{:S(2)}) copy-start(bf16[5,1152]{1,0:T(8,128)(2,1)} %img_hbm.1) | copy-start | bytes 34564
  2.7 0.7 %copy-start.1 = (bf16[5,1152]{1,0:T(8,128)(2,1)S(1)}, bf16[5,1152]{1,0:T(8,128)(2,1)}, u32[]{:S(2)}) copy-start(bf16[5,1152]{1,0:T(8,128)(2,1)} %txt_hbm.1) | copy-start | bytes 34564

commit v2 on v1

--- a/solution.py
+++ b/solution.py
@@ -22,19 +22,18 @@
 
 def kernel(
     n_img, n_txt,
-    img_hbm, txt_hbm, match_ref, temp_ref, bias_ref,
-    grad_img_ref, grad_txt_ref, loss_ref, dtemp_ref, dbias_ref,
-    img_in, txt_in, img_all, txt_all, img_part, txt_part, img_back, txt_back, sums,
-    in_sem, img_out, txt_out, txt_back_out, img_back_out, sums_out, img_sem, txt_sem, img_back_sem, txt_back_sem, sums_sem,
+    img_hbm, txt_hbm, match_hbm, temp_hbm, bias_hbm,
+    grad_img_ref, grad_txt_ref, totals_ref,
+    img_in, txt_in, match_ref, temp_ref, bias_ref, img_all, txt_all, img_part, txt_part, img_back, txt_back, sums, col_sums,
+    in_sem, img_out, txt_out, img_back_out, txt_back_out, sums_out, col_sums_out,
+    img_sem, txt_sem, img_back_sem, txt_back_sem, sums_sem, col_sums_sem,
 ):
     rows, width = img_in.shape
     n_z = n_txt // 2
     n_plane = n_img * 2
-    n_all = n_img * n_txt
     i = lax.axis_index("img")
     t = lax.axis_index("txt")
     z, core = t // 2, t % 2
-    me = i * n_txt + t
 
     def plane(k, sign):
         return (
@@ -45,24 +44,29 @@
     def column(k, sign):
         return (i, lax.rem(z + sign * k + n_z, n_z) * 2 + core)
 
-    def anyone(k):
-        other = lax.rem(me + k, n_all)
-        return (other // n_txt, lax.rem(other, n_txt))
-
     load_img = pltpu.make_async_copy(img_hbm, img_in, in_sem.at[0])
     load_txt = pltpu.make_async_copy(txt_hbm, txt_in, in_sem.at[1])
-    load_img.start()
-    load_txt.start()
+    small_loads = [
+        pltpu.make_async_copy(match_hbm, match_ref, in_sem.at[2]),
+        pltpu.make_async_copy(temp_hbm, temp_ref, in_sem.at[3]),
+        pltpu.make_async_copy(bias_hbm, bias_ref, in_sem.at[4]),
+    ]
+    for load in [load_img, load_txt] + small_loads:
+        load.start()
 
     barrier = pltpu.get_barrier_semaphore()
-    each(1, n_all, lambda k: pl.semaphore_signal(
-        barrier, inc=1, device_id=anyone(k), device_id_type=MESH))
+    each(1, n_z, lambda k: pl.semaphore_signal(
+        barrier, inc=1, device_id=column(k, 1), device_id_type=MESH))
+    each(1, n_plane, lambda k: pl.semaphore_signal(
+        barrier, inc=1, device_id=plane(k, 1), device_id_type=MESH))
 
     def unit_rows(ref):
         wide = ref[...].astype(jnp.float32)
         norm = jnp.sqrt(jnp.sum(wide * wide, axis=-1, keepdims=True) + 1e-06)
         return wide / norm, norm
 
+    for load in small_loads:
+        load.wait()
     load_img.wait()
     img_unit, img_norm = unit_rows(img_in)
     sub = lax.broadcasted_iota(jnp.int32, (PAD - rows, width), 0)
@@ -79,7 +83,7 @@
     txt_all[0] = jnp.concatenate(
         [txt_unit, jnp.zeros((PAD - rows, width), jnp.float32)], axis=0).astype(jnp.bfloat16)
 
-    pl.semaphore_wait(barrier, n_all - 1)
+    pl.semaphore_wait(barrier, n_z + n_plane - 2)
 
     def img_copy(k):
         return pltpu.make_async_remote_copy(
@@ -138,7 +142,14 @@
     def sums_copy(k):
         return pltpu.make_async_remote_copy(
             src_ref=sums.at[0], dst_ref=sums.at[k], send_sem=sums_out.at[k],
-            recv_sem=sums_sem.at[k], device_id=anyone(k), device_id_type=MESH)
+            recv_sem=sums_sem.at[k], device_id=plane(k, 1), device_id_type=MESH)
+
+    def col_sums_copy(k):
+        return pltpu.make_async_remote_copy(
+            src_ref=col_sums.at[0], dst_ref=col_sums.at[k], send_sem=col_sums_out.at[k],
+            recv_sem=col_sums_sem.at[k], device_id=column(k, 1), device_id_type=MESH)
+
+    each(1, n_plane, lambda k: sums_copy(k).start())
 
     weighted = (temper * slopes).astype(jnp.bfloat16)
     txt_term = lax.dot_general(
@@ -161,7 +172,10 @@
             recv_sem=img_back_sem.at[k], device_id=plane(k, -1), device_id_type=MESH)
 
     each(1, n_plane, lambda k: img_back_copy(k).start())
-    each(1, n_all, lambda k: sums_copy(k).start())
+
+    each(1, n_plane, lambda k: sums_copy(k).wait_recv())
+    col_sums[0] = jnp.sum(sums[...], axis=0)
+    each(1, n_z, lambda k: col_sums_copy(k).start())
 
     def unit_back(unit, norm, upstream):
         return (upstream - unit * jnp.sum(unit * upstream, axis=-1, keepdims=True)) / norm
@@ -175,60 +189,80 @@
     grad_img_unit = gather_sum(img_term[0:PAD], img_back, n_plane, img_back_copy)
     grad_img_ref[...] = unit_back(img_unit, img_norm, grad_img_unit)
 
-    each(1, n_all, lambda k: sums_copy(k).wait_recv())
-    batch = jnp.float32(rows * n_all)
-    totals = jnp.sum(sums[...], axis=0) / (batch * batch)
-    loss_ref[0] = jnp.sum(jnp.where(lane == 0, totals, 0.0))
-    dtemp_ref[0] = jnp.sum(jnp.where(lane == 1, totals, 0.0))
-    dbias_ref[0] = jnp.sum(jnp.where(lane == 2, totals, 0.0))
+    each(1, n_z, lambda k: col_sums_copy(k).wait_recv())
+    batch = jnp.float32(rows * n_img * n_txt)
+    totals_ref[...] = jnp.sum(col_sums[...], axis=0) / (batch * batch)
 
     each(1, n_z, lambda k: (txt_copy(k).wait_send(), txt_back_copy(k).wait_send()))
     each(1, n_plane, lambda k: (img_copy(k).wait_send(), img_back_copy(k).wait_send()))
-    each(1, n_all, lambda k: sums_copy(k).wait_send())
+    each(1, n_z, lambda k: col_sums_copy(k).wait_send())
+    each(1, n_plane, lambda k: sums_copy(k).wait_send())
+
+
+def finish(
+    grad_img_ref, grad_txt_ref, totals_ref,
+    grad_img_hbm, grad_txt_hbm, loss_hbm, dtemp_hbm, dbias_hbm, loss_ref, dtemp_ref, dbias_ref, sem,
+):
+    stores = [
+        pltpu.make_async_copy(grad_img_ref, grad_img_hbm, sem.at[0]),
+        pltpu.make_async_copy(grad_txt_ref, grad_txt_hbm, sem.at[1]),
+        pltpu.make_async_copy(loss_ref, loss_hbm, sem.at[2]),
+        pltpu.make_async_copy(dtemp_ref, dtemp_hbm, sem.at[3]),
+        pltpu.make_async_copy(dbias_ref, dbias_hbm, sem.at[4]),
+    ]
+    stores[0].start()
+    stores[1].start()
+    loss_ref[0] = totals_ref[0, 0]
+    dtemp_ref[0] = totals_ref[0, 1]
+    dbias_ref[0] = totals_ref[0, 2]
+    for store in stores[2:]:
+        store.start()
+    for store in stores:
+        store.wait()
 
 
 def solution(mesh):
     n_img, n_txt = mesh.shape["img"], mesh.shape["txt"]
-    n_z, n_plane, n_all = n_txt // 2, n_img * 2, n_img * n_txt
+    n_z, n_plane = n_txt // 2, n_img * 2
 
     def per_device(img_emb, txt_emb, match, log_temp, bias):
         rows, width = img_emb.shape
-        smem = pl.BlockSpec(memory_space=pltpu.SMEM)
         vmem = pl.BlockSpec(memory_space=pltpu.VMEM)
-        hbm = pl.BlockSpec(memory_space=pl.ANY)
+        hbm = pl.BlockSpec(memory_space=pltpu.HBM)
         one = jax.ShapeDtypeStruct((1,), jnp.float32)
         grad = jax.ShapeDtypeStruct((rows, width), jnp.float32)
         dma = pltpu.SemaphoreType.DMA
-        return pl.pallas_call(
+        parts = pl.pallas_call(
             functools.partial(kernel, n_img, n_txt),
-            out_shape=(grad, grad, one, one, one),
-            in_specs=[hbm, hbm, smem, smem, smem],
-            out_specs=(vmem, vmem, smem, smem, smem),
+            out_shape=(grad, grad, jax.ShapeDtypeStruct((1, 128), jnp.float32)),
+            in_specs=[hbm] * 5,
+            out_specs=(vmem,) * 3,
             scratch_shapes=[
                 pltpu.VMEM((rows, width), jnp.bfloat16),
                 pltpu.VMEM((rows, width), jnp.bfloat16),
+                pltpu.SMEM((rows,), jnp.int32),
+                pltpu.SMEM((1,), jnp.float32),
+                pltpu.SMEM((1,), jnp.float32),
                 pltpu.VMEM((n_plane, PAD, width), jnp.bfloat16),
                 pltpu.VMEM((n_z, PAD, width), jnp.bfloat16),
                 pltpu.VMEM((n_plane, PAD, width), jnp.bfloat16),
                 pltpu.VMEM((n_z, PAD, width), jnp.bfloat16),
                 pltpu.VMEM((n_plane, PAD, width), jnp.bfloat16),
                 pltpu.VMEM((n_z, PAD, width), jnp.bfloat16),
-                pltpu.VMEM((n_all, 1, 128), jnp.float32),
-                dma((2,)),
-                dma((n_plane,)),
-                dma((n_z,)),
-                dma((n_z,)),
-                dma((n_plane,)),
-                dma((n_all,)),
-                dma((n_plane,)),
-                dma((n_z,)),
-                dma((n_plane,)),
-                dma((n_z,)),
-                dma((n_all,)),
-            ],
+                pltpu.VMEM((n_plane, 1, 128), jnp.float32),
+                pltpu.VMEM((n_z, 1, 128), jnp.float32),
+                dma((5,)),
+            ] + [dma((n_plane,)), dma((n_z,))] * 6,
             compiler_params=pltpu.CompilerParams(
                 collective_id=0, has_side_effects=True, vmem_limit_bytes=40 * 1024 * 1024),
         )(img_emb, txt_emb, match, log_temp, bias)
+        return pl.pallas_call(
+            finish,
+            out_shape=(grad, grad, one, one, one),
+            in_specs=[vmem] * 3,
+            out_specs=(hbm,) * 5,
+            scratch_shapes=[pltpu.SMEM((1,), jnp.float32)] * 3 + [dma((5,))],
+        )(*parts)
 
     split = P(("img", "txt"), None)
     return jax.shard_map(

time: 28.5 us -> 24.6 us (0.86)
  between operations: 7.14 us -> 1.98 us
  Pallas kernels: 18.4 us -> 19.1 us
  local copies, waits for them, and re-layouts: 2.68 us -> 3.19 us
    pallas_call x0 -> x1, Pallas kernels: none -> 1.48 us  [per_device(): pl.pallas_call(finish, out_shape=(grad, grad, one, one, one), in_specs=[v...]
    pallas_call x1, Pallas kernels: 18.4 us -> 17.6 us  [per_device(): pl.pallas_call(functools.partial(kernel, n_img, n_txt), out_shape=(grad,...]
    unnamed x8 -> x12, local copies, waits for them, and re-layouts: 2.68 us -> 3.19 us
where the time goes in v2:
time: 24.6 us; the launch traced here: 24.3 us
  Pallas kernels  19.1 us (78%)
  local copies, waits for them, and re-layouts  3.19 us (13%)
  between operations  1.98 us (8%)
    pallas_call x1, Pallas kernels, per_device(): pl.pallas_call(functools.partial(kernel, n_img, n_txt), out_shape=(grad,...  17.6 us
    unnamed x12, local copies, waits for them, and re-layouts  3.19 us
    pallas_call x1, Pallas kernels, per_device(): pl.pallas_call(finish, out_shape=(grad, grad, one, one, one), in_specs=[v...  1.48 us

profile of v2, /device:TPU:0, one launch (start us, length us, event | category | flops | bytes accessed | tf_op | source)
XLA Modules:
  0.0 24.3 jit_solution(310264143725502227)
XLA Ops:
  1.3 0.0 copy-start.4
  1.9 0.0 copy-done.4
  2.0 0.0 copy-start.2
  2.0 0.7 %copy-done.2 = bf16[5,1152]{1,0:T(8,128)(2,1)S(1)} copy-done((bf16[5,1152]{1,0:T(8,128)(2,1)S(1)}, bf16[5,1152]{1,0:T(8,128)(2,1)}, u32[]{:S(2)}) %copy-start.2) | copy-done | bytes 11544
  2.7 0.0 copy-start.3
  2.7 0.7 %copy-done.3 = bf16[5,1152]{1,0:T(8,128)(2,1)S(1)} copy-done((bf16[5,1152]{1,0:T(8,128)(2,1)S(1)}, bf16[5,1152]{1,0:T(8,128)(2,1)}, u32[]{:S(2)}) %copy-start.3) | copy-done | bytes 11544
  3.4 17.6 %shard_map.92 = (f32[5,1152]{1,0:T(8,128)S(1)}, f32[5,1152]{1,0:T(8,128)S(1)}, f32[1,128]{1,0:T(1,128)S(1)}) custom-call(bf16[5,1152]{1,0:T(8,128)(2,1)S(1)} %copy-done.2, bf16[5,1152]{1,0:T(8,128)(2,1)S(1)} %copy-done.3, s32[5]{0:T(128)S(1)} %copy-done.4, f32[1]{0:T(128)S(6)} %copy.10.temp_hbm, f32[1]{0:T(128)S(6)} %copy.11.bias_hbm), custom_call_target="tpu_custom_call" | custom-call | tf_op jit(solution)/shard_map/pallas_call | solution.py:235
  21.1 0.0 copy-start
  21.1 0.6 %copy-done = f32[5,1152]{1,0:T(8,128)} copy-done((f32[5,1152]{1,0:T(8,128)}, f32[5,1152]{1,0:T(8,128)S(1)}, u32[]{:S(2)}) %copy-start) | copy-done | bytes 23064
  21.7 0.0 copy-start.1
  21.7 0.6 %copy-done.1 = f32[5,1152]{1,0:T(8,128)} copy-done((f32[5,1152]{1,0:T(8,128)}, f32[5,1152]{1,0:T(8,128)S(1)}, u32[]{:S(2)}) %copy-start.1) | copy-done | bytes 23064
  22.3 0.0 copy-start.5
  22.3 0.5 %copy-done.5 = f32[1,128]{1,0:T(1,128)} copy-done((f32[1,128]{1,0:T(1,128)}, f32[1,128]{1,0:T(1,128)S(1)}, u32[]{:S(2)}) %copy-start.5) | copy-done | bytes 536
  22.8 1.5 %shard_map.93 = (f32[5,1152]{1,0:T(8,128)}, f32[5,1152]{1,0:T(8,128)}, f32[1]{0:T(128)}, f32[1]{0:T(128)}, f32[1]{0:T(128)}) custom-call(f32[5,1152]{1,0:T(8,128)} %copy-done, f32[5,1152]{1,0:T(8,128)} %copy-done.1, f32[1,128]{1,0:T(1,128)} %copy-done.5), custom_call_target="tpu_custom_call" | custom-call | tf_op jit(solution)/shard_map/pallas_call | solution.py:259
Async XLA Ops:
  1.3 0.7 %copy-start.4 = (s32[5]{0:T(128)S(1)}, s32[5]{0:T(128)}, u32[]{:S(2)}) copy-start(s32[5]{0:T(128)} %match_hbm.1) | copy-start | bytes 64
  2.0 0.7 %copy-start.2 = (bf16[5,1152]{1,0:T(8,128)(2,1)S(1)}, bf16[5,1152]{1,0:T(8,128)(2,1)}, u32[]{:S(2)}) copy-start(bf16[5,1152]{1,0:T(8,128)(2,1)} %img_hbm.1) | copy-start | bytes 34564
  2.7 0.7 %copy-start.3 = (bf16[5,1152]{1,0:T(8,128)(2,1)S(1)}, bf16[5,1152]{1,0:T(8,128)(2,1)}, u32[]{:S(2)}) copy-start(bf16[5,1152]{1,0:T(8,128)(2,1)} %txt_hbm.1) | copy-start | bytes 34564
  21.1 0.6 %copy-start = (f32[5,1152]{1,0:T(8,128)}, f32[5,1152]{1,0:T(8,128)S(1)}, u32[]{:S(2)}) copy-start(f32[5,1152]{1,0:T(8,128)S(1)} %get-tuple-element.8.grad_img_ref) | copy-start | bytes 69124
  21.7 0.6 %copy-start.1 = (f32[5,1152]{1,0:T(8,128)}, f32[5,1152]{1,0:T(8,128)S(1)}, u32[]{:S(2)}) copy-start(f32[5,1152]{1,0:T(8,128)S(1)} %get-tuple-element.9.grad_txt_ref) | copy-start | bytes 69124
  22.3 0.5 %copy-start.5 = (f32[1,128]{1,0:T(1,128)}, f32[1,128]{1,0:T(1,128)S(1)}, u32[]{:S(2)}) copy-start(f32[1,128]{1,0:T(1,128)S(1)} %get-tuple-element.10.totals_ref) | copy-start | bytes 1540

commit v3 on v2

--- a/solution.py
+++ b/solution.py
@@ -232,9 +232,11 @@
         one = jax.ShapeDtypeStruct((1,), jnp.float32)
         grad = jax.ShapeDtypeStruct((rows, width), jnp.float32)
         dma = pltpu.SemaphoreType.DMA
+        img_emb, txt_emb, match = (
+            pltpu.with_memory_space_constraint(x, pltpu.HBM) for x in (img_emb, txt_emb, match))
         parts = pl.pallas_call(
             functools.partial(kernel, n_img, n_txt),
-            out_shape=(grad, grad, jax.ShapeDtypeStruct((1, 128), jnp.float32)),
+            out_shape=(pltpu.VMEM((rows, width), jnp.float32),) * 2 + (pltpu.VMEM((1, 128), jnp.float32),),
             in_specs=[hbm] * 5,
             out_specs=(vmem,) * 3,
             scratch_shapes=[

time: 24.6 us -> 23.1 us (0.939)
  local copies, waits for them, and re-layouts: 3.19 us -> 1.77 us
    unnamed x12 -> x6, local copies, waits for them, and re-layouts: 3.19 us -> 1.77 us
where the time goes in v3:
time: 23.1 us; the launch traced here: 22.8 us
  Pallas kernels  19.1 us (83%)
  between operations  1.94 us (8%)
  local copies, waits for them, and re-layouts  1.77 us (8%)
    pallas_call x1, Pallas kernels, per_device(): pl.pallas_call(functools.partial(kernel, n_img, n_txt), out_shape=(pltpu....  17.7 us
    unnamed x6, local copies, waits for them, and re-layouts  1.77 us
    pallas_call x1, Pallas kernels, per_device(): pl.pallas_call(finish, out_shape=(grad, grad, one, one, one), in_specs=[v...  1.48 us

profile of v3, /device:TPU:0, one launch (start us, length us, event | category | flops | bytes accessed | tf_op | source)
XLA Modules:
  0.0 22.8 jit_solution(8153156998969044243)
XLA Ops:
  1.9 17.7 %shard_map.92 = (f32[5,1152]{1,0:T(8,128)S(1)}, f32[5,1152]{1,0:T(8,128)S(1)}, f32[1,128]{1,0:T(1,128)S(1)}) custom-call(bf16[5,1152]{1,0:T(8,128)(2,1)} %img_hbm.1, bf16[5,1152]{1,0:T(8,128)(2,1)} %txt_hbm.1, s32[5]{0:T(128)} %match_hbm.1, f32[1]{0:T(128)S(6)} %copy.10.temp_hbm, f32[1]{0:T(128)S(6)} %copy.11.bias_hbm), custom_call_target="tpu_custom_call" | custom-call | tf_op jit(solution)/shard_map/pallas_call | solution.py:237
  19.6 0.0 copy-start
  19.6 0.6 %copy-done = f32[5,1152]{1,0:T(8,128)} copy-done((f32[5,1152]{1,0:T(8,128)}, f32[5,1152]{1,0:T(8,128)S(1)}, u32[]{:S(2)}) %copy-start) | copy-done | bytes 23064
  20.2 0.0 copy-start.1
  20.2 0.6 %copy-done.1 = f32[5,1152]{1,0:T(8,128)} copy-done((f32[5,1152]{1,0:T(8,128)}, f32[5,1152]{1,0:T(8,128)S(1)}, u32[]{:S(2)}) %copy-start.1) | copy-done | bytes 23064
  20.8 0.0 copy-start.2
  20.8 0.6 %copy-done.2 = f32[1,128]{1,0:T(1,128)} copy-done((f32[1,128]{1,0:T(1,128)}, f32[1,128]{1,0:T(1,128)S(1)}, u32[]{:S(2)}) %copy-start.2) | copy-done | bytes 536
  21.4 1.5 %shard_map.93 = (f32[5,1152]{1,0:T(8,128)}, f32[5,1152]{1,0:T(8,128)}, f32[1]{0:T(128)}, f32[1]{0:T(128)}, f32[1]{0:T(128)}) custom-call(f32[5,1152]{1,0:T(8,128)} %copy-done, f32[5,1152]{1,0:T(8,128)} %copy-done.1, f32[1,128]{1,0:T(1,128)} %copy-done.2), custom_call_target="tpu_custom_call" | custom-call | tf_op jit(solution)/shard_map/pallas_call | solution.py:261
Async XLA Ops:
  19.6 0.6 %copy-start = (f32[5,1152]{1,0:T(8,128)}, f32[5,1152]{1,0:T(8,128)S(1)}, u32[]{:S(2)}) copy-start(f32[5,1152]{1,0:T(8,128)S(1)} %get-tuple-element.8.grad_img_ref) | copy-start | bytes 69124
  20.2 0.6 %copy-start.1 = (f32[5,1152]{1,0:T(8,128)}, f32[5,1152]{1,0:T(8,128)S(1)}, u32[]{:S(2)}) copy-start(f32[5,1152]{1,0:T(8,128)S(1)} %get-tuple-element.9.grad_txt_ref) | copy-start | bytes 69124
  20.8 0.6 %copy-start.2 = (f32[1,128]{1,0:T(1,128)}, f32[1,128]{1,0:T(1,128)S(1)}, u32[]{:S(2)}) copy-start(f32[1,128]{1,0:T(1,128)S(1)} %get-tuple-element.10.totals_ref) | copy-start | bytes 1540

commit v4 on v3

--- a/solution.py
+++ b/solution.py
@@ -44,6 +44,10 @@
     def column(k, sign):
         return (i, lax.rem(z + sign * k + n_z, n_z) * 2 + core)
 
+    def anyone(k):
+        other = lax.rem(i * n_txt + t + k, n_img * n_txt)
+        return (other // n_txt, lax.rem(other, n_txt))
+
     load_img = pltpu.make_async_copy(img_hbm, img_in, in_sem.at[0])
     load_txt = pltpu.make_async_copy(txt_hbm, txt_in, in_sem.at[1])
     small_loads = [
@@ -55,10 +59,8 @@
         load.start()
 
     barrier = pltpu.get_barrier_semaphore()
-    each(1, n_z, lambda k: pl.semaphore_signal(
-        barrier, inc=1, device_id=column(k, 1), device_id_type=MESH))
-    each(1, n_plane, lambda k: pl.semaphore_signal(
-        barrier, inc=1, device_id=plane(k, 1), device_id_type=MESH))
+    each(1, n_img * n_txt, lambda k: pl.semaphore_signal(
+        barrier, inc=1, device_id=anyone(k), device_id_type=MESH))
 
     def unit_rows(ref):
         wide = ref[...].astype(jnp.float32)
@@ -83,7 +85,7 @@
     txt_all[0] = jnp.concatenate(
         [txt_unit, jnp.zeros((PAD - rows, width), jnp.float32)], axis=0).astype(jnp.bfloat16)
 
-    pl.semaphore_wait(barrier, n_z + n_plane - 2)
+    pl.semaphore_wait(barrier, n_img * n_txt - 1)
 
     def img_copy(k):
         return pltpu.make_async_remote_copy(
@@ -142,14 +144,14 @@
     def sums_copy(k):
         return pltpu.make_async_remote_copy(
             src_ref=sums.at[0], dst_ref=sums.at[k], send_sem=sums_out.at[k],
-            recv_sem=sums_sem.at[k], device_id=plane(k, 1), device_id_type=MESH)
+            recv_sem=sums_sem.at[k], device_id=anyone(k), device_id_type=MESH)
 
     def col_sums_copy(k):
         return pltpu.make_async_remote_copy(
             src_ref=col_sums.at[0], dst_ref=col_sums.at[k], send_sem=col_sums_out.at[k],
             recv_sem=col_sums_sem.at[k], device_id=column(k, 1), device_id_type=MESH)
 
-    each(1, n_plane, lambda k: sums_copy(k).start())
+    each(1, n_img * n_txt, lambda k: sums_copy(k).start())
 
     weighted = (temper * slopes).astype(jnp.bfloat16)
     txt_term = lax.dot_general(
@@ -173,9 +175,6 @@
 
     each(1, n_plane, lambda k: img_back_copy(k).start())
 
-    each(1, n_plane, lambda k: sums_copy(k).wait_recv())
-    col_sums[0] = jnp.sum(sums[...], axis=0)
-    each(1, n_z, lambda k: col_sums_copy(k).start())
 
     def unit_back(unit, norm, upstream):
         return (upstream - unit * jnp.sum(unit * upstream, axis=-1, keepdims=True)) / norm
@@ -189,14 +188,13 @@
     grad_img_unit = gather_sum(img_term[0:PAD], img_back, n_plane, img_back_copy)
     grad_img_ref[...] = unit_back(img_unit, img_norm, grad_img_unit)
 
-    each(1, n_z, lambda k: col_sums_copy(k).wait_recv())
+    each(1, n_img * n_txt, lambda k: sums_copy(k).wait_recv())
     batch = jnp.float32(rows * n_img * n_txt)
-    totals_ref[...] = jnp.sum(col_sums[...], axis=0) / (batch * batch)
+    totals_ref[...] = jnp.sum(sums[...], axis=0) / (batch * batch)
 
     each(1, n_z, lambda k: (txt_copy(k).wait_send(), txt_back_copy(k).wait_send()))
     each(1, n_plane, lambda k: (img_copy(k).wait_send(), img_back_copy(k).wait_send()))
-    each(1, n_z, lambda k: col_sums_copy(k).wait_send())
-    each(1, n_plane, lambda k: sums_copy(k).wait_send())
+    each(1, n_img * n_txt, lambda k: sums_copy(k).wait_send())
 
 
 def finish(
@@ -251,16 +249,17 @@
                 pltpu.VMEM((n_z, PAD, width), jnp.bfloat16),
                 pltpu.VMEM((n_plane, PAD, width), jnp.bfloat16),
                 pltpu.VMEM((n_z, PAD, width), jnp.bfloat16),
-                pltpu.VMEM((n_plane, 1, 128), jnp.float32),
+                pltpu.VMEM((n_img * n_txt, 1, 128), jnp.float32),
                 pltpu.VMEM((n_z, 1, 128), jnp.float32),
                 dma((5,)),
-            ] + [dma((n_plane,)), dma((n_z,))] * 6,
+            ] + ([dma((n_plane,)), dma((n_z,))] * 2 + [dma((n_img * n_txt,)), dma((n_z,))]) * 2,
             compiler_params=pltpu.CompilerParams(
-                collective_id=0, has_side_effects=True, vmem_limit_bytes=40 * 1024 * 1024),
+                collective_id=0, has_side_effects=True, vmem_limit_bytes=16 * 1024 * 1024),
         )(img_emb, txt_emb, match, log_temp, bias)
         return pl.pallas_call(
             finish,
             out_shape=(grad, grad, one, one, one),
+            compiler_params=pltpu.CompilerParams(vmem_limit_bytes=4 * 1024 * 1024),
             in_specs=[vmem] * 3,
             out_specs=(hbm,) * 5,
             scratch_shapes=[pltpu.SMEM((1,), jnp.float32)] * 3 + [dma((5,))],

time: 23.1 us -> 20 us (0.87)
  local copies, waits for them, and re-layouts: 1.77 us -> 0 us
  Pallas kernels: 19.1 us -> 17.9 us
    unnamed x6 -> x0, local copies, waits for them, and re-layouts: 1.77 us -> none
    pallas_call x1, Pallas kernels: 1.48 us -> 0.7 us  [per_device(): pl.pallas_call(finish, out_shape=(grad, grad, one, one, one), compiler_pa...]
    pallas_call x1, Pallas kernels: 17.7 us -> 17.2 us  [per_device(): pl.pallas_call(functools.partial(kernel, n_img, n_txt), out_shape=(pltpu....]
where the time goes in v4:
time: 20 us; the launch traced here: 19.8 us
  Pallas kernels  17.9 us (89%)
  between operations  1.93 us (10%)
    pallas_call x1, Pallas kernels, per_device(): pl.pallas_call(functools.partial(kernel, n_img, n_txt), out_shape=(pltpu....  17.2 us
    pallas_call x1, Pallas kernels, per_device(): pl.pallas_call(finish, out_shape=(grad, grad, one, one, one), compiler_pa...  0.7 us

profile of v4, /device:TPU:0, one launch (start us, length us, event | category | flops | bytes accessed | tf_op | source)
XLA Modules:
  0.0 19.8 jit_solution(11914947778788494745)
XLA Ops:
  1.9 17.2 %shard_map.92 = (f32[5,1152]{1,0:T(8,128)S(1)}, f32[5,1152]{1,0:T(8,128)S(1)}, f32[1,128]{1,0:T(1,128)S(1)}) custom-call(bf16[5,1152]{1,0:T(8,128)(2,1)} %img_hbm.1, bf16[5,1152]{1,0:T(8,128)(2,1)} %txt_hbm.1, s32[5]{0:T(128)} %match_hbm.1, f32[1]{0:T(128)S(6)} %copy.10.temp_hbm, f32[1]{0:T(128)S(6)} %copy.11.bias_hbm), custom_call_target="tpu_custom_call" | custom-call | tf_op jit(solution)/shard_map/pallas_call | solution.py:235
  19.1 0.7 %shard_map.93 = (f32[5,1152]{1,0:T(8,128)}, f32[5,1152]{1,0:T(8,128)}, f32[1]{0:T(128)}, f32[1]{0:T(128)}, f32[1]{0:T(128)}) custom-call(f32[5,1152]{1,0:T(8,128)S(1)} %get-tuple-element.8.grad_img_ref, f32[5,1152]{1,0:T(8,128)S(1)} %get-tuple-element.9.grad_txt_ref, f32[1,128]{1,0:T(1,128)S(1)} %get-tuple-element.10.totals_ref), custom_call_target="tpu_custom_call" | custom-call | tf_op jit(solution)/shard_map/pallas_call | solution.py:259

commit v5 on v4

--- a/solution.py
+++ b/solution.py
@@ -24,9 +24,9 @@
     n_img, n_txt,
     img_hbm, txt_hbm, match_hbm, temp_hbm, bias_hbm,
     grad_img_ref, grad_txt_ref, totals_ref,
-    img_in, txt_in, match_ref, temp_ref, bias_ref, img_all, txt_all, img_part, txt_part, img_back, txt_back, sums, col_sums,
-    in_sem, img_out, txt_out, img_back_out, txt_back_out, sums_out, col_sums_out,
-    img_sem, txt_sem, img_back_sem, txt_back_sem, sums_sem, col_sums_sem,
+    img_in, txt_in, match_ref, temp_ref, bias_ref, img_all, txt_all, img_part, txt_part, img_back, txt_back, sums,
+    in_sem, img_out, txt_out, img_back_out, txt_back_out, sums_out,
+    img_sem, txt_sem, img_back_sem, txt_back_sem, sums_sem,
 ):
     rows, width = img_in.shape
     n_z = n_txt // 2
@@ -35,18 +35,25 @@
     t = lax.axis_index("txt")
     z, core = t // 2, t % 2
 
+    def wrap(value, n):
+        return jnp.where(value >= n, value - n, value)
+
+    def shift(value, k, sign, n):
+        return wrap(value + k, n) if sign > 0 else wrap(value + (n - k), n)
+
     def plane(k, sign):
-        return (
-            lax.rem(i + sign * (k // 2) + n_img, n_img),
-            z * 2 + lax.rem(core + k, 2),
-        )
+        flip = k % 2
+        return (shift(i, k // 2, sign, n_img), z * 2 + core + flip * (1 - 2 * core))
 
     def column(k, sign):
-        return (i, lax.rem(z + sign * k + n_z, n_z) * 2 + core)
+        return (i, shift(z, k, sign, n_z) * 2 + core)
 
     def anyone(k):
-        other = lax.rem(i * n_txt + t + k, n_img * n_txt)
-        return (other // n_txt, lax.rem(other, n_txt))
+        return (shift(i, k // n_txt, 1, n_img), shift(t, k % n_txt, 1, n_txt))
+
+    def wait_all(ref, n, sem):
+        slots = ref.at[pl.ds(1, n - 1)]
+        pltpu.make_async_copy(slots, slots, sem.at[0]).wait()
 
     load_img = pltpu.make_async_copy(img_hbm, img_in, in_sem.at[0])
     load_txt = pltpu.make_async_copy(txt_hbm, txt_in, in_sem.at[1])
@@ -89,19 +96,19 @@
 
     def img_copy(k):
         return pltpu.make_async_remote_copy(
-            src_ref=img_all.at[0], dst_ref=img_all.at[k], send_sem=img_out.at[k],
-            recv_sem=img_sem.at[k], device_id=plane(k, 1), device_id_type=MESH)
+            src_ref=img_all.at[0], dst_ref=img_all.at[k], send_sem=img_out.at[0],
+            recv_sem=img_sem.at[0], device_id=plane(k, 1), device_id_type=MESH)
 
     def txt_copy(k):
         return pltpu.make_async_remote_copy(
-            src_ref=txt_all.at[0], dst_ref=txt_all.at[k], send_sem=txt_out.at[k],
-            recv_sem=txt_sem.at[k], device_id=column(k, 1), device_id_type=MESH)
+            src_ref=txt_all.at[0], dst_ref=txt_all.at[k], send_sem=txt_out.at[0],
+            recv_sem=txt_sem.at[0], device_id=column(k, 1), device_id_type=MESH)
 
     each(1, n_z, lambda k: txt_copy(k).start())
     each(1, n_plane, lambda k: img_copy(k).start())
 
-    each(1, n_z, lambda k: txt_copy(k).wait_recv())
-    each(1, n_plane, lambda k: img_copy(k).wait_recv())
+    wait_all(txt_all, n_z, txt_sem)
+    wait_all(img_all, n_plane, img_sem)
 
     n_rows, n_cols = n_plane * PAD, n_z * PAD
     img_rows = img_all[...].astype(jnp.float32).reshape(n_rows, width).astype(jnp.bfloat16)
@@ -143,13 +150,8 @@
 
     def sums_copy(k):
         return pltpu.make_async_remote_copy(
-            src_ref=sums.at[0], dst_ref=sums.at[k], send_sem=sums_out.at[k],
-            recv_sem=sums_sem.at[k], device_id=anyone(k), device_id_type=MESH)
-
-    def col_sums_copy(k):
-        return pltpu.make_async_remote_copy(
-            src_ref=col_sums.at[0], dst_ref=col_sums.at[k], send_sem=col_sums_out.at[k],
-            recv_sem=col_sums_sem.at[k], device_id=column(k, 1), device_id_type=MESH)
+            src_ref=sums.at[0], dst_ref=sums.at[k], send_sem=sums_out.at[0],
+            recv_sem=sums_sem.at[0], device_id=anyone(k), device_id_type=MESH)
 
     each(1, n_img * n_txt, lambda k: sums_copy(k).start())
 
@@ -160,8 +162,8 @@
 
     def txt_back_copy(k):
         return pltpu.make_async_remote_copy(
-            src_ref=txt_part.at[k], dst_ref=txt_back.at[k], send_sem=txt_back_out.at[k],
-            recv_sem=txt_back_sem.at[k], device_id=column(k, -1), device_id_type=MESH)
+            src_ref=txt_part.at[k], dst_ref=txt_back.at[k], send_sem=txt_back_out.at[0],
+            recv_sem=txt_back_sem.at[0], device_id=column(k, -1), device_id_type=MESH)
 
     each(1, n_z, lambda k: txt_back_copy(k).start())
 
@@ -170,8 +172,8 @@
 
     def img_back_copy(k):
         return pltpu.make_async_remote_copy(
-            src_ref=img_part.at[k], dst_ref=img_back.at[k], send_sem=img_back_out.at[k],
-            recv_sem=img_back_sem.at[k], device_id=plane(k, -1), device_id_type=MESH)
+            src_ref=img_part.at[k], dst_ref=img_back.at[k], send_sem=img_back_out.at[0],
+            recv_sem=img_back_sem.at[0], device_id=plane(k, -1), device_id_type=MESH)
 
     each(1, n_plane, lambda k: img_back_copy(k).start())
 
@@ -179,22 +181,24 @@
     def unit_back(unit, norm, upstream):
         return (upstream - unit * jnp.sum(unit * upstream, axis=-1, keepdims=True)) / norm
 
-    def gather_sum(own, back, n, copy):
-        each(1, n, lambda k: copy(k).wait_recv())
+    def gather_sum(own, back, n, sem):
+        wait_all(back, n, sem)
         return (own + jnp.sum(back[1:].astype(jnp.float32), axis=0))[0:rows]
 
-    grad_txt_unit = gather_sum(txt_term[0:PAD], txt_back, n_z, txt_back_copy)
+    grad_txt_unit = gather_sum(txt_term[0:PAD], txt_back, n_z, txt_back_sem)
     grad_txt_ref[...] = unit_back(txt_unit, txt_norm, grad_txt_unit)
-    grad_img_unit = gather_sum(img_term[0:PAD], img_back, n_plane, img_back_copy)
+    grad_img_unit = gather_sum(img_term[0:PAD], img_back, n_plane, img_back_sem)
     grad_img_ref[...] = unit_back(img_unit, img_norm, grad_img_unit)
 
-    each(1, n_img * n_txt, lambda k: sums_copy(k).wait_recv())
+    wait_all(sums, n_img * n_txt, sums_sem)
     batch = jnp.float32(rows * n_img * n_txt)
     totals_ref[...] = jnp.sum(sums[...], axis=0) / (batch * batch)
 
-    each(1, n_z, lambda k: (txt_copy(k).wait_send(), txt_back_copy(k).wait_send()))
-    each(1, n_plane, lambda k: (img_copy(k).wait_send(), img_back_copy(k).wait_send()))
-    each(1, n_img * n_txt, lambda k: sums_copy(k).wait_send())
+    wait_all(txt_all, n_z, txt_out)
+    wait_all(img_all, n_plane, img_out)
+    wait_all(txt_back, n_z, txt_back_out)
+    wait_all(img_back, n_plane, img_back_out)
+    wait_all(sums, n_img * n_txt, sums_out)
 
 
 def finish(
@@ -250,9 +254,8 @@
                 pltpu.VMEM((n_plane, PAD, width), jnp.bfloat16),
                 pltpu.VMEM((n_z, PAD, width), jnp.bfloat16),
                 pltpu.VMEM((n_img * n_txt, 1, 128), jnp.float32),
-                pltpu.VMEM((n_z, 1, 128), jnp.float32),
                 dma((5,)),
-            ] + ([dma((n_plane,)), dma((n_z,))] * 2 + [dma((n_img * n_txt,)), dma((n_z,))]) * 2,
+            ] + [dma((1,))] * 10,
             compiler_params=pltpu.CompilerParams(
                 collective_id=0, has_side_effects=True, vmem_limit_bytes=16 * 1024 * 1024),
         )(img_emb, txt_emb, match, log_temp, bias)

time: 20 us -> 18.9 us (0.945)
  Pallas kernels: 17.9 us -> 16.8 us
    pallas_call x1, Pallas kernels: 17.2 us -> 16.1 us  [per_device(): pl.pallas_call(functools.partial(kernel, n_img, n_txt), out_shape=(pltpu....]
where the time goes in v5:
time: 18.9 us; the launch traced here: 18.7 us
  Pallas kernels  16.8 us (89%)
  between operations  1.93 us (10%)
    pallas_call x1, Pallas kernels, per_device(): pl.pallas_call(functools.partial(kernel, n_img, n_txt), out_shape=(pltpu....  16.1 us
    pallas_call x1, Pallas kernels, per_device(): pl.pallas_call(finish, out_shape=(grad, grad, one, one, one), compiler_pa...  0.7 us

profile of v5, /device:TPU:0, one launch (start us, length us, event | category | flops | bytes accessed | tf_op | source)
XLA Modules:
  0.0 18.7 jit_solution(16380886188327331190)
XLA Ops:
  1.9 16.1 %shard_map.92 = (f32[5,1152]{1,0:T(8,128)S(1)}, f32[5,1152]{1,0:T(8,128)S(1)}, f32[1,128]{1,0:T(1,128)S(1)}) custom-call(bf16[5,1152]{1,0:T(8,128)(2,1)} %img_hbm.1, bf16[5,1152]{1,0:T(8,128)(2,1)} %txt_hbm.1, s32[5]{0:T(128)} %match_hbm.1, f32[1]{0:T(128)S(6)} %copy.10.temp_hbm, f32[1]{0:T(128)S(6)} %copy.11.bias_hbm), custom_call_target="tpu_custom_call" | custom-call | tf_op jit(solution)/shard_map/pallas_call | solution.py:239
  18.0 0.7 %shard_map.93 = (f32[5,1152]{1,0:T(8,128)}, f32[5,1152]{1,0:T(8,128)}, f32[1]{0:T(128)}, f32[1]{0:T(128)}, f32[1]{0:T(128)}) custom-call(f32[5,1152]{1,0:T(8,128)S(1)} %get-tuple-element.8.grad_img_ref, f32[5,1152]{1,0:T(8,128)S(1)} %get-tuple-element.9.grad_txt_ref, f32[1,128]{1,0:T(1,128)S(1)} %get-tuple-element.10.totals_ref), custom_call_target="tpu_custom_call" | custom-call | tf_op jit(solution)/shard_map/pallas_call | solution.py:262
